TPU v7x, 32 devices: a whole 2x2x4 slice. The times are simulated.
32 devices in a mesh: grp: 2 (over y), wide: 4 (over z), narrow: 4 (over x, core).
Axes of the slice: x: 2, y: 2, z: 4, core: 2. Of those that a mesh axis runs over, the one named last changes fastest.
Arguments:
- voltages: bfloat16 [8, 256, 81920], P(('grp', 'narrow'), 'wide'), parts along dimension 0, may hold values from -16 to 16
- fir_coeffs: float32 [4, 16384], replicated, may hold values from -0.5 to 3
- channel_keep_flags: int32 [16384], P(('grp', 'wide')), parts along dimension 0, may hold values 0 or 1
Outputs:
- visibilities: bfloat16 [128, 2, 4, 256, 1024], P(('grp', 'wide'), None, 'narrow'), parts along dimension 0
There are 2 independent parts, one for each index of `grp`. A program takes and returns all parts, laid end to end along the dimension named above; an argument that names none is the same for every part. Nothing has to cross between parts.
All inputs are finite; a program needn't handle non-finite values. No bound on the sum of `channel_keep_flags` on one device may be relied on, other than what follows from the above.
Results may differ from a plain program's by a relative error of at most 0.006.
Values may be sent and summed in bfloat16 or wider, within the bound.
A program may use at most 128 MiB of HBM per device.

v0:
```python
import jax
import jax.numpy as jnp
from jax import lax
from jax.sharding import PartitionSpec as P

FACTOR_A = 128


def phase_table(length, outputs, period):
    left_index = jnp.arange(length, dtype=jnp.int32)
    right_index = jnp.arange(outputs, dtype=jnp.int32)
    product = left_index[:, None] * right_index[None, :] % period
    radians = product.astype(jnp.float32) * (2.0 * jnp.pi / period)
    return (jnp.cos(radians), jnp.sin(radians))


def correlate(own_rows, incoming, norm_divisor):
    return (
        jnp.einsum("doqisc,dqmsc->doim", own_rows, incoming, preferred_element_type=jnp.float32)
        * norm_divisor
    )


def body(voltages, fir_coeffs, channel_keep_flags):
    tap_count, frame_len = fir_coeffs.shape
    inputs_here = voltages.shape[1]
    spectrum_count = voltages.shape[2] // frame_len - tap_count + 1
    factor_b = frame_len // FACTOR_A
    blocks = voltages[0].reshape(inputs_here, spectrum_count + tap_count - 1, frame_len)
    filtered = jnp.zeros((inputs_here, spectrum_count, frame_len), jnp.float32)
    for tap_index in range(tap_count):
        filtered = filtered + fir_coeffs[tap_index] * blocks[
            :, tap_index : tap_index + spectrum_count
        ].astype(jnp.float32)
    rounded = lax.optimization_barrier(filtered.astype(jnp.bfloat16))
    folded = rounded.reshape(inputs_here, spectrum_count, FACTOR_A, factor_b)
    high = lax.Precision.HIGHEST
    first_cos, first_sin = phase_table(FACTOR_A, FACTOR_A, FACTOR_A)
    first_table = jnp.stack([first_cos, -first_sin], axis=1)
    table_high = first_table.astype(jnp.bfloat16)
    table_low = (first_table - table_high.astype(jnp.float32)).astype(jnp.bfloat16)
    first_pass = jnp.einsum(
        "psab,aqc->psbqc", folded, table_high, preferred_element_type=jnp.float32
    )
    first_pass = first_pass + jnp.einsum(
        "psab,aqc->psbqc", folded, table_low, preferred_element_type=jnp.float32
    )
    twist_cos, twist_sin = phase_table(factor_b, FACTOR_A, frame_len)
    real_part = first_pass[:, :, :, 0] * twist_cos + first_pass[:, :, :, 1] * twist_sin
    imag_part = first_pass[:, :, :, 1] * twist_cos - first_pass[:, :, :, 0] * twist_sin
    twisted = jnp.stack([real_part, imag_part], axis=3)
    last_cos, last_sin = phase_table(factor_b, factor_b // 2, factor_b)
    cos_rows = last_cos.T
    sin_rows = last_sin.T
    last_table = jnp.stack(
        [jnp.stack([cos_rows, sin_rows], axis=1), jnp.stack([-sin_rows, cos_rows], axis=1)], axis=1
    )
    channel_spectra = jnp.einsum("dqrb,psbrc->dqpsc", last_table, twisted, precision=high)
    channel_spectra = (channel_spectra * frame_len ** (-0.5)).astype(jnp.bfloat16)
    turned = lax.all_to_all(channel_spectra, "wide", split_axis=0, concat_axis=2, tiled=True)
    local_bins = turned.shape[0]
    bin_width = turned.shape[4]
    flag_block = channel_keep_flags.astype(jnp.bfloat16).reshape(local_bins, 1, 1, 1, bin_width)
    weighted = turned * flag_block
    rotated = jnp.stack([weighted[:, 1], -weighted[:, 0]], axis=1)
    own_rows = jnp.stack([weighted, rotated], axis=1)
    norm_divisor = 1.0 / (spectrum_count * bin_width)
    gathered = correlate(
        own_rows, lax.all_gather(turned, "narrow", axis=2, tiled=True), norm_divisor
    )
    result = gathered.astype(jnp.bfloat16)
    return result[:, :, None]


def solution(mesh):
    placed = (P(("grp", "narrow"), "wide", None), P(), P(("grp", "wide")))
    return jax.shard_map(
        body,
        mesh=mesh,
        in_specs=placed,
        out_specs=P(("grp", "wide"), None, "narrow", None, None),
        check_vma=False,
    )
```

profile of v0, /device:TPU:17, one launch (start us, length us, event | category | flops | bytes accessed | tf_op | source)
XLA Modules:
  0.0 365.1 jit_solution(15743999849120088472)
XLA Ops:
  6.5 0.0 all-gather.2.cloned.1.call-start
  6.5 0.1 fusion.44
  6.7 0.1 fusion.42
  6.8 0.3 fusion.36
  7.1 0.3 sine_negate_fusion
  7.4 1.8 fusion.50
  9.2 18.7 %reshape_squeeze.3 = bf16[64,5,16384]{2,1,0:T(8,128)(2,1)} reshape(bf16[1,64,81920]{2,1,0:T(8,128)(2,1)} %param.3) | data formatting | bytes 20971520 | tf_op jit(solution)/shard_map/reshape;squeeze | solution.py:29
  28.0 37.0 %fusion.48 = (bf16[64,2,16384]{2,1,0:T(2,128)(2,1)}, bf16[64,2,16384]{2,1,0:T(2,128)(2,1)}, bf16[64,2,16384]{2,1,0:T(2,128)(2,1)}, bf16[64,2,16384]{2,1,0:T(2,128)(2,1)}) fusion(bf16[64,5,16384]{2,1,0:T(8,128)(2,1)} %reshape_squeeze.3), kind=kLoop, calls=%fused_computation.72 | loop fusion | bytes 33554432 | tf_op jit(solution)/shard_map/slice | solution.py:32
  65.0 17.7 %add_convert_fusion = bf16[64,2,16384]{2,0,1:T(8,128)(2,1)S(1)} fusion(bf16[64,2,16384]{2,1,0:T(2,128)(2,1)} %get-tuple-element.10, bf16[64,2,16384]{2,1,0:T(2,128)(2,1)} %get-tuple-element.8, bf16[64,2,16384]{2,1,0:T(2,128)(2,1)} %get-tuple-element.9, bf16[64,2,16384]{2,1,0:T(2,128)(2,1)} %get-tuple-element.7, f32[16384]{0:T(1024)S(1)} %bitcast.80, ...), kind=kLoop, calls=%fused_computation.16 | loop fusion | flops 25165824 | bytes 21233664 | tf_op jit(solution)/shard_map/convert_element_type | solution.py:35
  82.7 1.2 copy.48
  83.9 8.5 %fusion.12 = f32[64,2,128,2,128]{4,2,3,1,0:T(8,128)} fusion(bf16[64,2,128,128,1]{3,2,0,1,4:T(8,128)(2,1)S(1)} %bitcast.74, f32[128,1,128]{2,0,1:T(8,128)S(1)} %get-tuple-element.19, f32[128,1,128]{2,0,1:T(8,128)S(1)} %get-tuple-element.20), kind=kOutput, calls=%fused_computation.20 | convolution fusion | flops 1073872896 | bytes 21102592 | tf_op jit(solution)/shard_map/psab,aqc->psbqc/dot_general | solution.py:42
  92.5 14.3 %convolution_add_fusion = f32[64,2,128,2,128]{4,2,3,1,0:T(8,128)} fusion(f32[64,2,128,2,128]{4,2,3,1,0:T(8,128)} %fusion.12, bf16[64,2,128,128,1]{3,2,0,1,4:T(8,128)(2,1)S(1)} %bitcast.75, f32[128,1,128]{2,0,1:T(8,128)S(1)} %get-tuple-element.19, f32[128,1,128]{2,0,1:T(8,128)S(1)} %get-tuple-element.20), kind=kOutput, calls=%fused_computation.9 | convolution fusion | flops 1078099968 | bytes 37879808 | tf_op jit(solution)/shard_map/psab,aqc->psbqc/dot_general | solution.py:45
  106.8 7.2 %multiply_add_fusion = (f32[64,2,128,1,128]{4,2,3,1,0:T(8,128)S(1)}, f32[64,2,128,1,128]{4,2,3,1,0:T(8,128)S(1)}) fusion(f32[64,2,128,2,128]{4,2,3,1,0:T(8,128)} %convolution_add_fusion, f32[128,128]{1,0:T(8,128)S(1)} %get-tuple-element.21, f32[128,128]{1,0:T(8,128)S(1)} %get-tuple-element.22), kind=kLoop, calls=%fused_computation.15 | loop fusion | flops 12582912 | bytes 33685504 | tf_op jit(solution)/shard_map/add | solution.py:49
  113.9 10.8 %fusion.9 = bf16[64,2,64,2,128]{4,0,3,2,1:T(8,128)(2,1)S(1)} fusion(f32[64,2,128,1,128]{4,2,3,1,0:T(8,128)S(1)} %get-tuple-element.6, f32[64,2,128,1,128]{4,2,3,1,0:T(8,128)S(1)} %get-tuple-element.5, f32[64,1,2,128]{3,0,2,1:T(8,128)S(1)} %get-tuple-element.18, f32[64,1,2,128]{3,0,2,1:T(8,128)S(1)} %get-tuple-element.17), kind=kOutput, calls=%fused_computation.12 | convolution fusion | flops 6450872320 | bytes 21102592 | tf_op jit(solution)/shard_map/dqrb,psbrc->dqpsc/dot_general | solution.py:58
  124.7 6.3 %copy.28 = bf16[64,2,64,2,128]{4,3,2,1,0:T(2,128)(2,1)} copy(bf16[64,2,64,2,128]{4,0,3,2,1:T(8,128)(2,1)S(1)} %fusion.9) | data formatting | bytes 8388608 | tf_op jit(solution)/shard_map/convert_element_type | solution.py:59
  131.0 95.1 %all_to_all.21 = bf16[64,2,64,2,128]{4,3,2,1,0:T(2,128)(2,1)S(1)} all-to-all(bf16[64,2,64,2,128]{4,3,2,1,0:T(2,128)(2,1)} %copy.28), channel_id=1, replica_groups=mesh['grp'=2,'wide'=4,'narrow'=4] {'wide'}, dimensions={0} | all-to-all | bytes 8388608 | tf_op jit(solution)/shard_map/all_to_all | solution.py:60
  226.1 0.0 copy-start.1
  226.1 3.1 copy.29
  229.3 0.0 all-gather.2.cloned.1.call-update
  229.3 0.0 copy-done.1
  229.3 2.5 broadcast_multiply_fusion
  231.8 0.0 copy-start
  231.8 0.4 fusion.49
  232.2 2.3 maximum_bitcast_fusion.2
  234.5 0.6 copy-done
  235.1 2.5 bitcast_multiply_fusion.2
  237.6 100.3 %all-gather.2.cloned.1.call-done = bf16[16,2,1024,2,128]{4,2,3,1,0:T(8,128)(2,1)} async-done(((bf16[16,2,256,2,128]{4,2,3,1,0:T(8,128)(2,1)}), bf16[16,2,1024,2,128]{4,2,3,1,0:T(8,128)(2,1)}) %all-gather.2.cloned.1.call-update) | async-done | bytes 16777232 | tf_op jit(solution)/shard_map/all_gather | solution.py:69
  337.9 20.3 %fusion.1 = bf16[16,2,1,256,1024]{4,3,2,1,0:T(8,128)(2,1)} fusion(bf16[16,2,1024,2,128]{4,2,3,1,0:T(8,128)(2,1)} %all-gather.2.cloned.1.call-done, bf16[16,1,2,256,2,128]{5,3,4,2,0,1:T(8,128)(2,1)} %maximum_bitcast_fusion.2, bf16[16,1,2,256,2,128]{5,3,4,2,0,1:T(8,128)(2,1)} %bitcast_multiply_fusion.2), kind=kOutput, calls=%fused_computation.2 | convolution fusion | flops 8610906112 | bytes 41943040 | tf_op jit(solution)/shard_map/doqisc,dqmsc->doim/dot_general | solution.py:19
  (2 shorter events, 0.0 us)
Async XLA Ops:
  6.5 331.4 %all-gather.2.cloned.1.call-start = ((), (), s32[]{:S(2)}) async-start(), calls=%async_computation.1 | async-start | bytes 20971520 | tf_op jit(solution)/shard_map/all_gather | solution.py:69
  226.1 3.2 copy-start.1
  231.8 3.3 copy-start
Sparse Core Ops, SparseCore 0:
  229.4 108.4 all-gather.1
where the time goes:
time: 367 us; the launch traced here: 365 us
  waiting for transfers between devices  100 us (27%)
  blocking collectives  95.1 us (26%)
  local copies, waits for them, and re-layouts  68.9 us (19%)
  matrix products  53.9 us (15%)
  other arithmetic  33.4 us (9%)
  between operations  13.5 us (4%)
    all_gather x1, waiting for transfers between devices, body(): lax.all_gather(turned, 'narrow', axis=2, tiled=True)  100 us
    all_to_all x1, blocking collectives, body(): lax.all_to_all(channel_spectra, 'wide', split_axis=0, concat_axis=2, tile...  95.1 us
    slice x1, local copies, waits for them, and re-layouts, body(): blocks[:, tap_index:tap_index + spectrum_count].astype(jnp.float32)  37 us
    dot_general x1, matrix products, correlate(): jnp.einsum('doqisc,dqmsc->doim', own_rows, incoming, preferred_element_ty...  20.3 us
    another operation x1, local copies, waits for them, and re-layouts, body(): voltages[0].reshape(inputs_here, spectrum_count + tap_count - 1, frame_len)  18.7 us
    convert_element_type x1, other arithmetic, body(): rounded = lax.optimization_barrier(filtered.astype(jnp.bfloat16))  17.7 us
    dot_general x1, matrix products, body(): jnp.einsum('psab,aqc->psbqc', folded, table_low, preferred_element_type=j...  14.3 us
    dot_general x1, matrix products, body(): jnp.einsum('dqrb,psbrc->dqpsc', last_table, twisted, precision=high)  10.8 us
  transfers between devices with their start and end apart: 1, of which 1 were waited for; matrix products, arithmetic and copies ran while one was open for 2% of the time, Pallas kernels for 0%

commit v1 on v0

--- a/solution.py
+++ b/solution.py
@@ -1,6 +1,11 @@
+import functools
+
 import jax
 import jax.numpy as jnp
+import numpy as np
 from jax import lax
+from jax.experimental import pallas as pl
+from jax.experimental.pallas import tpu as pltpu
 from jax.sharding import PartitionSpec as P
 
 FACTOR_A = 128
@@ -21,7 +26,7 @@
     )
 
 
-def body(voltages, fir_coeffs, channel_keep_flags):
+def plain_body(voltages, fir_coeffs, channel_keep_flags):
     tap_count, frame_len = fir_coeffs.shape
     inputs_here = voltages.shape[1]
     spectrum_count = voltages.shape[2] // frame_len - tap_count + 1
@@ -72,7 +77,157 @@
     return result[:, :, None]
 
 
+ROWS = 16
+
+
+def split_table(table):
+    high = table.astype(jnp.bfloat16)
+    low = (table - high.astype(np.float64)).astype(jnp.bfloat16)
+    return high, low
+
+
+def dft_tables(frame_len):
+    side = FACTOR_A
+    index = np.arange(side)
+    turn = 2.0 * np.pi * (np.outer(index, index) % side) / side
+    first = np.concatenate([np.cos(turn), -np.sin(turn)], axis=0)
+    first = np.concatenate(split_table(first), axis=1)
+    twist = 2.0 * np.pi * np.outer(index, index) / frame_len
+    twist = np.stack([np.cos(twist), np.sin(twist)]).astype(np.float32)
+    last_cos, last_sin = np.cos(turn[: side // 2]), np.sin(turn[: side // 2])
+    real_row = np.concatenate([last_cos, last_sin], axis=1)
+    imag_row = np.concatenate([-last_sin, last_cos], axis=1)
+    last = np.stack([real_row, imag_row], axis=1).reshape(side, 2 * side)
+    last = last * frame_len ** (-0.5)
+    last = np.concatenate(split_table(last), axis=0)
+    return first, twist, last
+
+
+def dft_rows(spectra_in, row, first_ref, twist_ref, last_ref, flip):
+    side = FACTOR_A
+    samples = jnp.concatenate([ref[row] for ref in spectra_in], axis=1)
+    samples = jnp.concatenate([samples, samples], axis=0)
+    first_pass = jnp.dot(first_ref[...], samples, preferred_element_type=jnp.float32)
+    twisted = []
+    for s in range(len(spectra_in)):
+        real = first_pass[:side, s * side : (s + 1) * side]
+        imag = first_pass[side:, s * side : (s + 1) * side]
+        cos, sin = twist_ref[0], twist_ref[1]
+        twisted.append(
+            jnp.concatenate([real * cos + imag * sin, imag * cos - real * sin], axis=1)
+        )
+    twisted = jnp.concatenate(twisted, axis=0).astype(jnp.bfloat16)
+    both = lax.dot_general(
+        last_ref[...], twisted, (((1,), (1,)), ((), ())), preferred_element_type=jnp.float32
+    )
+    total = both[:side] + both[side:]
+    start = pl.multiple_of(lax.rem(row, ROWS) * side, side)
+    for s in range(len(spectra_in)):
+        flip[s, pl.ds(start, side), :] = total[:, s * side : (s + 1) * side]
+
+
+def dft_kernel(x0_ref, x1_ref, first_ref, twist_ref, last_ref, out_ref, flip):
+    side = FACTOR_A
+
+    def one(row, carry):
+        dft_rows((x0_ref, x1_ref), row, first_ref, twist_ref, last_ref, flip)
+        return carry
+
+    lax.fori_loop(0, ROWS, one, 0, unroll=4)
+    for dq in range(side):
+        for s in range(2):
+            out_ref[dq, :, s * side : (s + 1) * side] = flip[
+                s, pl.ds(dq, ROWS, stride=side), :
+            ].astype(jnp.bfloat16)
+
+
+def dft(blocks, frame_len):
+    first, twist, last = dft_tables(frame_len)
+    rows, side = blocks[0].shape[0], FACTOR_A
+    whole = lambda *shape: pl.BlockSpec(shape, lambda i: (0,) * len(shape))
+    return pl.pallas_call(
+        dft_kernel,
+        grid=(rows // ROWS,),
+        in_specs=[pl.BlockSpec((ROWS, side, side), lambda i: (i, 0, 0))] * 2
+        + [whole(2 * side, 2 * side), whole(2, side, side), whole(2 * side, 2 * side)],
+        out_specs=pl.BlockSpec((side, ROWS, 2 * side), lambda i: (0, i, 0)),
+        out_shape=jax.ShapeDtypeStruct((side, rows, 2 * side), jnp.bfloat16),
+        scratch_shapes=[pltpu.VMEM((2, ROWS * side, side), jnp.float32)],
+        compiler_params=pltpu.CompilerParams(vmem_limit_bytes=40 * 2**20),
+    )(*blocks, jnp.asarray(first), jnp.asarray(twist), jnp.asarray(last))
+
+
+def correlate_kernel(scale, rows, flag_ref, all_ref, out_ref):
+    start = pl.multiple_of(lax.axis_index("narrow") * rows, rows)
+    flags = flag_ref[0]
+    own_real = all_ref[0, 0, pl.ds(start, rows), :] * flags
+    own_imag = all_ref[0, 1, pl.ds(start, rows), :] * flags
+    columns = jnp.concatenate([all_ref[0, 0], all_ref[0, 1]], axis=1)
+    for part, own in enumerate(((own_real, own_imag), (own_imag, -own_real))):
+        total = lax.dot_general(
+            jnp.concatenate(own, axis=1),
+            columns,
+            (((1,), (1,)), ((), ())),
+            preferred_element_type=jnp.float32,
+        )
+        out_ref[0, part, 0] = (total * scale).astype(jnp.bfloat16)
+
+
+def correlate_bins(gathered, flags, rows, scale):
+    bins, parts, inputs, depth = gathered.shape
+    return pl.pallas_call(
+        functools.partial(correlate_kernel, scale, rows),
+        grid=(bins,),
+        in_specs=[
+            pl.BlockSpec((1, 1, depth), lambda b: (b, 0, 0)),
+            pl.BlockSpec((1, parts, inputs, depth), lambda b: (b, 0, 0, 0)),
+        ],
+        out_specs=pl.BlockSpec((1, parts, 1, rows, inputs), lambda b: (b, 0, 0, 0, 0)),
+        out_shape=jax.ShapeDtypeStruct((bins, parts, 1, rows, inputs), jnp.bfloat16),
+        compiler_params=pltpu.CompilerParams(vmem_limit_bytes=40 * 2**20),
+    )(flags, gathered)
+
+
+def filter_rows(voltages, fir_coeffs, spectrum):
+    frame_len = fir_coeffs.shape[1]
+    total = 0.0
+    for tap_index in range(fir_coeffs.shape[0]):
+        start = (spectrum + tap_index) * frame_len
+        block = voltages[:, start : start + frame_len].astype(jnp.float32)
+        total = total + fir_coeffs[tap_index] * block
+    return total.astype(jnp.bfloat16)
+
+
+def fast_body(wide, voltages, fir_coeffs, channel_keep_flags):
+    tap_count, frame_len = fir_coeffs.shape
+    inputs_here = voltages.shape[1]
+    spectrum_count = voltages.shape[2] // frame_len - tap_count + 1
+    bin_width = FACTOR_A
+    local_bins = channel_keep_flags.shape[0] // bin_width
+    filtered = [filter_rows(voltages[0], fir_coeffs, s) for s in range(spectrum_count)]
+    blocks = [lax.optimization_barrier(x).reshape(inputs_here, FACTOR_A, FACTOR_A) for x in filtered]
+    spectra = dft(blocks, frame_len).reshape(wide * local_bins, 2, inputs_here, 2 * bin_width)
+    turned = lax.all_to_all(spectra, "wide", split_axis=0, concat_axis=2, tiled=True)
+    gathered = lax.all_gather(turned, "narrow", axis=2, tiled=True)
+    flags = channel_keep_flags.astype(jnp.bfloat16).reshape(local_bins, 1, bin_width)
+    flags = jnp.concatenate([flags] * spectrum_count, axis=2)
+    scale = 1.0 / (spectrum_count * bin_width)
+    return correlate_bins(gathered, flags, wide * inputs_here, scale)
+
+
 def solution(mesh):
+    wide = mesh.shape["wide"]
+    narrow = mesh.shape["narrow"]
+
+    def body(voltages, fir_coeffs, channel_keep_flags):
+        tap_count, frame_len = fir_coeffs.shape
+        rows = voltages.shape[1]
+        spectrum_count = voltages.shape[2] // frame_len - tap_count + 1
+        fits = frame_len == FACTOR_A**2 and rows % ROWS == 0 and spectrum_count == 2
+        if fits and narrow == 4:
+            return fast_body(wide, voltages, fir_coeffs, channel_keep_flags)
+        return plain_body(voltages, fir_coeffs, channel_keep_flags)
+
     placed = (P(("grp", "narrow"), "wide", None), P(), P(("grp", "wide")))
     return jax.shard_map(
         body,

time: 367 us -> 266 us (0.72)
  local copies, waits for them, and re-layouts: 68.9 us -> 6 us
  matrix products: 53.9 us -> 0 us
  Pallas kernels: 0 us -> 36.1 us
  other arithmetic: 33.4 us -> 5.41 us
  waiting for transfers between devices: 100 us -> 108 us
    dot_general x4 -> x0, matrix products: 53.9 us -> none  [the longest x1 20.3 us: correlate(): jnp.einsum('doqisc,dqmsc->doim', own_rows, incoming, preferred_element_ty...]
    slice x2 -> x1, local copies, waits for them, and re-layouts: 38.9 us -> 1.82 us  [filter_rows(): total = total + fir_coeffs[tap_index] * block]
    pallas_call x0 -> x2, Pallas kernels: none -> 36.1 us  [the longest x1 20.8 us: correlate_bins(): pl.pallas_call(functools.partial(correlate_kernel, scale, rows), grid=(bi...]
    another operation x1 -> x0, local copies, waits for them, and re-layouts: 18.7 us -> none  [body(): voltages[0].reshape(inputs_here, spectrum_count + tap_count - 1, frame_len)]
    convert_element_type x1, other arithmetic: 17.7 us -> 5.39 us  [filter_rows(): return total.astype(jnp.bfloat16)]
    all_gather x1, waiting for transfers between devices: 100 us -> 108 us  [fast_body(): gathered = lax.all_gather(turned, 'narrow', axis=2, tiled=True)]
    add x1 -> x0, other arithmetic: 7.15 us -> none  [body(): first_pass[:, :, :, 0] * twist_cos + first_pass[:, :, :, 1] * twist_sin]
    convert_element_type x1 -> x0, local copies, waits for them, and re-layouts: 6.33 us -> none  [body(): (channel_spectra * frame_len ** (-0.5)).astype(jnp.bfloat16)]
  transfers between devices with their start and end apart: 1 -> 1, of which waited for: 1 -> 1; matrix products, arithmetic and copies ran while one was open for 2% -> 0% of each run, Pallas kernels for 0% -> 0%
where the time goes in v1:
time: 266 us; the launch traced here: 264 us
  waiting for transfers between devices  108 us (41%)
  blocking collectives  94.9 us (36%)
  Pallas kernels  36.1 us (14%)
  between operations  13.5 us (5%)
  local copies, waits for them, and re-layouts  6 us (2%)
  other arithmetic  5.41 us (2%)
    all_gather x1, waiting for transfers between devices, fast_body(): gathered = lax.all_gather(turned, 'narrow', axis=2, tiled=True)  108 us
    all_to_all x1, blocking collectives, fast_body(): lax.all_to_all(spectra, 'wide', split_axis=0, concat_axis=2, tiled=True)  94.9 us
    pallas_call x1, Pallas kernels, correlate_bins(): pl.pallas_call(functools.partial(correlate_kernel, scale, rows), grid=(bi...  20.8 us
    pallas_call x1, Pallas kernels, dft(): pl.pallas_call(dft_kernel, grid=(rows // ROWS,), in_specs=[pl.BlockSpec((...  15.3 us
    convert_element_type x1, other arithmetic, filter_rows(): return total.astype(jnp.bfloat16)  5.39 us
  transfers between devices with their start and end apart: 1, of which 1 were waited for; matrix products, arithmetic and copies ran while one was open for 0% of the time, Pallas kernels for 0%

profile of v1, /device:TPU:17, one launch (start us, length us, event | category | flops | bytes accessed | tf_op | source)
XLA Modules:
  0.0 263.8 jit_solution(9541225991390108932)
XLA Ops:
  6.5 0.0 all-gather.2.cloned.1.call-start
  6.5 1.8 fusion.8
  8.4 5.4 %fusion.7 = (bf16[64,16384]{1,0:T(8,128)(2,1)S(1)}, bf16[64,16384]{1,0:T(8,128)(2,1)S(1)}) fusion(bf16[64,81920]{1,0:T(8,128)(2,1)} %bitcast.21, f32[16384]{0:T(1024)S(1)} %bitcast.26, f32[16384]{0:T(1024)S(1)} %bitcast.27, f32[16384]{0:T(1024)S(1)} %bitcast.25, f32[16384]{0:T(1024)S(1)} %bitcast.24), kind=kLoop, calls=%fused_computation.13 | loop fusion | flops 22020096 | bytes 14942208 | tf_op jit(solution)/shard_map/convert_element_type | solution.py:198
  13.8 0.0 copy-start
  13.8 0.0 copy-start.1
  13.8 0.0 copy-start.2
  13.8 0.6 copy.11
  14.4 0.6 copy.10
  15.0 0.0 copy-done
  15.0 0.0 copy-done.1
  15.0 0.0 copy-done.2
  15.0 15.3 %shard_map.64 = bf16[128,64,256]{2,1,0:T(8,128)(2,1)S(1)} custom-call(bf16[64,128,128]{2,1,0:T(8,128)(2,1)S(1)} %bitcast.18, bf16[64,128,128]{2,1,0:T(8,128)(2,1)S(1)} %bitcast.17, bf16[256,256]{1,0:T(8,128)(2,1)S(1)} %copy-done.2, f32[2,128,128]{2,1,0:T(8,128)S(1)} %copy-done.1, bf16[256,256]{1,0:T(8,128)(2,1)S(1)} %copy-done), custom_call_target="tpu_custom_call" | custom-call | tf_op jit(solution)/shard_map/pallas_call | solution.py:148
  30.3 94.9 %all_to_all.18 = bf16[64,2,64,256]{3,2,1,0:T(8,128)(2,1)S(1)} all-to-all(bf16[64,2,64,256]{3,2,1,0:T(8,128)(2,1)S(1)} %bitcast.16), channel_id=1, replica_groups=mesh['grp'=2,'wide'=4,'narrow'=4] {'wide'}, dimensions={0} | all-to-all | bytes 8388608 | tf_op jit(solution)/shard_map/all_to_all | solution.py:210
  125.2 2.3 copy.9
  127.5 0.0 copy-start.3
  127.5 0.0 all-gather.2.cloned.1.call-update
  127.5 0.7 copy-done.3
  128.2 107.9 %all-gather.2.cloned.1.call-done.all_ref = bf16[16,2,1024,256]{3,2,1,0:T(8,128)(2,1)} async-done(((bf16[16,2,256,256]{3,2,1,0:T(8,128)(2,1)}), bf16[16,2,1024,256]{3,2,1,0:T(8,128)(2,1)}) %all-gather.2.cloned.1.call-update) | async-done | bytes 16777232 | tf_op jit(solution)/shard_map/all_gather | solution.py:211
  236.2 20.8 %shard_map.65 = bf16[16,2,1,256,1024]{4,3,2,1,0:T(8,128)(2,1)} custom-call(bf16[16,1,256]{2,1,0:T(2,128)(2,1)S(1)} %pad_maximum_fusion.flag_ref, bf16[16,2,1024,256]{3,2,1,0:T(8,128)(2,1)} %all-gather.2.cloned.1.call-done.all_ref), custom_call_target="tpu_custom_call" | custom-call | tf_op jit(solution)/shard_map/pallas_call | solution.py:178
  (3 shorter events, 0.0 us)
Async XLA Ops:
  6.5 229.6 %all-gather.2.cloned.1.call-start = ((), (), s32[]{:S(2)}) async-start(), calls=%async_computation.1 | async-start | bytes 20971520 | tf_op jit(solution)/shard_map/all_gather | solution.py:211
  13.8 1.2 copy-start
  13.8 1.2 copy-start.1
  13.8 1.2 copy-start.2
  127.5 0.7 copy-start.3
Sparse Core Ops, SparseCore 0:
  127.7 108.4 all-gather.1

commit v2 on v1

--- a/solution.py
+++ b/solution.py
@@ -78,6 +78,8 @@
 
 
 ROWS = 16
+CHUNKS = 8
+ORDER = (2, 1, 3)
 
 
 def split_table(table):
@@ -188,6 +190,121 @@
     )(flags, gathered)
 
 
+def move_kernel(wide, chunks, spectra, gathered, local_sem, z_send, z_recv, x_send, x_recv,
+                pair_send, pair_recv, last_send, last_recv):
+    me = lax.axis_index("wide")
+    panel = lax.axis_index("narrow")
+    pair = panel + 1 - 2 * lax.rem(panel, 2)
+    across = lax.rem(panel + 2, 4)
+    across_pair = lax.rem(pair + 2, 4)
+    rows = spectra.shape[3]
+    size = spectra.shape[1] // chunks
+
+    barrier = pltpu.get_barrier_semaphore()
+    peers = [{"wide": lax.rem(me + step, wide)} for step in range(1, wide)]
+    peers += [{"narrow": pair}, {"narrow": across}]
+    for peer in peers:
+        pl.semaphore_signal(barrier, inc=1, device_id=peer, device_id_type=pl.DeviceIdType.MESH)
+    pl.semaphore_wait(barrier, len(peers))
+
+    def spot(chunk, owner, source):
+        start = pl.multiple_of((owner * wide + source) * rows, rows)
+        return gathered.at[pl.ds(chunk * size, size), :, pl.ds(start, rows), :]
+
+    def mine(target, chunk):
+        return spectra.at[target, pl.ds(chunk * size, size)]
+
+    def remote(src, dst, send, recv, peer):
+        return pltpu.make_async_remote_copy(
+            src_ref=src, dst_ref=dst, send_sem=send, recv_sem=recv,
+            device_id=peer, device_id_type=pl.DeviceIdType.MESH,
+        )
+
+    def along(chunk, step):
+        target = lax.rem(me + step, wide)
+        return remote(mine(target, chunk), spot(chunk, panel, me), z_send.at[chunk, step],
+                      z_recv.at[chunk, step], {"wide": target})
+
+    def arriving(chunk, step):
+        source = lax.rem(me + wide - step, wide)
+        return remote(mine(me, chunk), spot(chunk, panel, source), z_send.at[chunk, step],
+                      z_recv.at[chunk, step], {"wide": source})
+
+    def block_at(chunk, step, owner):
+        return spot(chunk, owner, lax.rem(me + wide - step, wide))
+
+    def first_hop(chunk, step, to_pair, receiving=False):
+        owner = (pair if to_pair else across) if receiving else panel
+        dst = block_at(chunk, step, owner)
+        src = mine(me, chunk) if step == 0 else block_at(chunk, step, panel)
+        send, recv = (pair_send, pair_recv) if to_pair else (x_send, x_recv)
+        return remote(src, dst, send.at[chunk, step], recv.at[chunk, step],
+                      {"narrow": pair if to_pair else across})
+
+    def second_hop(chunk, step, receiving=False):
+        block = block_at(chunk, step, across_pair if receiving else across)
+        return remote(block, block, last_send.at[chunk, step], last_recv.at[chunk, step],
+                      {"narrow": pair})
+
+    def begin(chunk, carry):
+        first_hop(chunk, 0, False).start()
+        for step in ORDER:
+            along(chunk, step).start()
+        first_hop(chunk, 0, True).start()
+        pltpu.make_async_copy(mine(me, chunk), spot(chunk, panel, me), local_sem.at[chunk]).start()
+        return carry
+
+    def onward(chunk, carry):
+        for step in range(1, wide):
+            arriving(chunk, step).wait_recv()
+            first_hop(chunk, step, False).start()
+            first_hop(chunk, step, True).start()
+        return carry
+
+    def relay(chunk, carry):
+        for step in range(wide):
+            first_hop(chunk, step, False, True).wait_recv()
+            second_hop(chunk, step).start()
+        return carry
+
+    def both(chunk, carry):
+        onward(chunk, carry)
+        relay(chunk - 1, carry)
+        return carry
+
+    def finish(chunk, carry):
+        pltpu.make_async_copy(mine(me, chunk), spot(chunk, panel, me), local_sem.at[chunk]).wait()
+        for step in range(wide):
+            if step > 0:
+                along(chunk, step).wait_send()
+            first_hop(chunk, step, False).wait_send()
+            first_hop(chunk, step, True).wait_send()
+            first_hop(chunk, step, True, True).wait_recv()
+            second_hop(chunk, step).wait_send()
+            second_hop(chunk, step, True).wait_recv()
+        return carry
+
+    lax.fori_loop(0, chunks, begin, 0)
+    onward(0, 0)
+    lax.fori_loop(1, chunks, both, 0)
+    relay(chunks - 1, 0)
+    lax.fori_loop(0, chunks, finish, 0)
+
+
+def move(spectra, wide, narrow):
+    bins, parts, rows, depth = spectra.shape[1:]
+    chunks = CHUNKS
+    table = pltpu.SemaphoreType.DMA((chunks, wide))
+    return pl.pallas_call(
+        functools.partial(move_kernel, wide, chunks),
+        in_specs=[pl.BlockSpec(memory_space=pl.ANY)],
+        out_specs=pl.BlockSpec(memory_space=pl.ANY),
+        out_shape=jax.ShapeDtypeStruct((bins, parts, narrow * wide * rows, depth), jnp.bfloat16),
+        scratch_shapes=[pltpu.SemaphoreType.DMA((chunks,))] + [table] * 8,
+        compiler_params=pltpu.CompilerParams(collective_id=0, has_side_effects=True),
+    )(spectra)
+
+
 def filter_rows(voltages, fir_coeffs, spectrum):
     frame_len = fir_coeffs.shape[1]
     total = 0.0
@@ -206,9 +323,8 @@
     local_bins = channel_keep_flags.shape[0] // bin_width
     filtered = [filter_rows(voltages[0], fir_coeffs, s) for s in range(spectrum_count)]
     blocks = [lax.optimization_barrier(x).reshape(inputs_here, FACTOR_A, FACTOR_A) for x in filtered]
-    spectra = dft(blocks, frame_len).reshape(wide * local_bins, 2, inputs_here, 2 * bin_width)
-    turned = lax.all_to_all(spectra, "wide", split_axis=0, concat_axis=2, tiled=True)
-    gathered = lax.all_gather(turned, "narrow", axis=2, tiled=True)
+    spectra = dft(blocks, frame_len).reshape(wide, local_bins, 2, inputs_here, 2 * bin_width)
+    gathered = move(spectra, wide, 4)
     flags = channel_keep_flags.astype(jnp.bfloat16).reshape(local_bins, 1, bin_width)
     flags = jnp.concatenate([flags] * spectrum_count, axis=2)
     scale = 1.0 / (spectrum_count * bin_width)
@@ -224,7 +340,8 @@
         rows = voltages.shape[1]
         spectrum_count = voltages.shape[2] // frame_len - tap_count + 1
         fits = frame_len == FACTOR_A**2 and rows % ROWS == 0 and spectrum_count == 2
-        if fits and narrow == 4:
+        bins_fit = channel_keep_flags.shape[0] // FACTOR_A % CHUNKS == 0
+        if fits and bins_fit and narrow == 4 and wide == 4:
             return fast_body(wide, voltages, fir_coeffs, channel_keep_flags)
         return plain_body(voltages, fir_coeffs, channel_keep_flags)
 

time: 266 us -> 164 us (0.62)
  Pallas kernels: 36.1 us -> 153 us
  waiting for transfers between devices: 108 us -> 0 us
  blocking collectives: 94.9 us -> 0 us
  between operations: 13.5 us -> 0.11 us
    pallas_call x0 -> x1, Pallas kernels: none -> 116 us  [move(): pl.pallas_call(functools.partial(move_kernel, wide, chunks), in_specs=[pl...]
    all_gather x1 -> x0, waiting for transfers between devices: 108 us -> none  [fast_body(): gathered = lax.all_gather(turned, 'narrow', axis=2, tiled=True)]
    all_to_all x1 -> x0, blocking collectives: 94.9 us -> none  [fast_body(): lax.all_to_all(spectra, 'wide', split_axis=0, concat_axis=2, tiled=True)]
  transfers between devices with their start and end apart: 1 -> 0, of which waited for: 1 -> 0; matrix products, arithmetic and copies ran while one was open for 0% -> 0% of each run, Pallas kernels for 0% -> 0%
where the time goes in v2:
time: 164 us
  Pallas kernels  153 us (93%)
  other arithmetic  6.11 us (4%)
  local copies, waits for them, and re-layouts  5.01 us (3%)
    pallas_call x1, Pallas kernels, move(): pl.pallas_call(functools.partial(move_kernel, wide, chunks), in_specs=[pl...  116 us
    pallas_call x1, Pallas kernels, correlate_bins(): pl.pallas_call(functools.partial(correlate_kernel, scale, rows), grid=(bi...  20.8 us
    pallas_call x1, Pallas kernels, dft(): pl.pallas_call(dft_kernel, grid=(rows // ROWS,), in_specs=[pl.BlockSpec((...  15.3 us
    convert_element_type x1, other arithmetic, filter_rows(): return total.astype(jnp.bfloat16)  5.39 us

profile of v2, /device:TPU:17, one launch (start us, length us, event | category | flops | bytes accessed | tf_op | source)
XLA Modules:
  0.0 163.8 jit_solution(8064647250099825033)
XLA Ops:
  0.0 0.7 convert_bitcast_fusion
  0.7 1.8 %fusion.8 = (f32[1,16384]{1,0:T(1,128)S(1)}, f32[1,16384]{1,0:T(1,128)S(1)}, f32[1,16384]{1,0:T(1,128)S(1)}, f32[1,16384]{1,0:T(1,128)S(1)}) fusion(f32[4,16384]{1,0:T(4,128)} %param.7), kind=kLoop, calls=%fused_computation.16 | loop fusion | bytes 524288 | tf_op jit(solution)/shard_map/slice | solution.py:314
  2.6 5.4 %fusion.7 = (bf16[64,16384]{1,0:T(8,128)(2,1)S(1)}, bf16[64,16384]{1,0:T(8,128)(2,1)S(1)}) fusion(bf16[64,81920]{1,0:T(8,128)(2,1)} %bitcast.15, f32[16384]{0:T(1024)S(1)} %bitcast.20, f32[16384]{0:T(1024)S(1)} %bitcast.21, f32[16384]{0:T(1024)S(1)} %bitcast.19, f32[16384]{0:T(1024)S(1)} %bitcast.18), kind=kLoop, calls=%fused_computation.13 | loop fusion | flops 22020096 | bytes 14942208 | tf_op jit(solution)/shard_map/convert_element_type | solution.py:315
  8.0 0.0 copy-start.1
  8.0 0.0 copy-start.2
  8.0 0.0 copy-start.3
  8.0 0.6 copy.10
  8.6 0.6 copy.9
  9.2 0.0 copy-done.1
  9.2 0.0 copy-done.2
  9.2 0.0 copy-done.3
  9.2 15.3 %shard_map.64 = bf16[128,64,256]{2,1,0:T(8,128)(2,1)S(1)} custom-call(bf16[64,128,128]{2,1,0:T(8,128)(2,1)S(1)} %bitcast.14, bf16[64,128,128]{2,1,0:T(8,128)(2,1)S(1)} %bitcast.13, bf16[256,256]{1,0:T(8,128)(2,1)S(1)} %copy-done.3, f32[2,128,128]{2,1,0:T(8,128)S(1)} %copy-done.2, bf16[256,256]{1,0:T(8,128)(2,1)S(1)} %copy-done.1), custom_call_target="tpu_custom_call" | custom-call | tf_op jit(solution)/shard_map/pallas_call | solution.py:150
  24.5 0.0 copy-start
  24.5 2.0 %copy-done = bf16[128,64,256]{2,1,0:T(8,128)(2,1)} copy-done((bf16[128,64,256]{2,1,0:T(8,128)(2,1)}, bf16[128,64,256]{2,1,0:T(8,128)(2,1)S(1)}, u32[]{:S(2)}) %copy-start) | copy-done | bytes 4194328
  26.5 116.5 %shard_map.65.all_ref = bf16[16,2,1024,256]{3,2,1,0:T(8,128)(2,1)} custom-call(bf16[4,16,2,64,256]{4,3,2,1,0:T(8,128)(2,1)} %bitcast.12), custom_call_target="tpu_custom_call" | custom-call | tf_op jit(solution)/shard_map/pallas_call | solution.py:298
  143.0 20.8 %shard_map.66 = bf16[16,2,1,256,1024]{4,3,2,1,0:T(8,128)(2,1)} custom-call(bf16[16,1,256]{2,1,0:T(2,128)(2,1)S(1)} %pad_maximum_fusion.flag_ref, bf16[16,2,1024,256]{3,2,1,0:T(8,128)(2,1)} %shard_map.65.all_ref), custom_call_target="tpu_custom_call" | custom-call | tf_op jit(solution)/shard_map/pallas_call | solution.py:180
  (2 shorter events, 0.0 us)
Async XLA Ops:
  8.0 1.2 copy-start.1
  8.0 1.2 copy-start.2
  8.0 1.2 copy-start.3
  24.5 2.0 %copy-start = (bf16[128,64,256]{2,1,0:T(8,128)(2,1)}, bf16[128,64,256]{2,1,0:T(8,128)(2,1)S(1)}, u32[]{:S(2)}) copy-start(bf16[128,64,256]{2,1,0:T(8,128)(2,1)S(1)} %shard_map.64) | copy-start | bytes 12582916

commit v3 on v2

--- a/solution.py
+++ b/solution.py
@@ -78,7 +78,7 @@
 
 
 ROWS = 16
-CHUNKS = 8
+GROUPS = 4
 ORDER = (2, 1, 3)
 
 
@@ -128,35 +128,21 @@
         flip[s, pl.ds(start, side), :] = total[:, s * side : (s + 1) * side]
 
 
-def dft_kernel(x0_ref, x1_ref, first_ref, twist_ref, last_ref, out_ref, flip):
+def dft_chunk(spectra_in, chunk, tables, flip, spectra):
     side = FACTOR_A
+    _, wide, bins, parts, _, _ = spectra.shape
 
     def one(row, carry):
-        dft_rows((x0_ref, x1_ref), row, first_ref, twist_ref, last_ref, flip)
+        dft_rows(spectra_in, chunk * ROWS + row, *tables, flip)
         return carry
 
     lax.fori_loop(0, ROWS, one, 0, unroll=4)
     for dq in range(side):
-        for s in range(2):
-            out_ref[dq, :, s * side : (s + 1) * side] = flip[
+        target, bin_index, part = dq // (bins * parts), dq // parts % bins, dq % parts
+        for s in range(len(spectra_in)):
+            spectra[chunk, target, bin_index, part, :, s * side : (s + 1) * side] = flip[
                 s, pl.ds(dq, ROWS, stride=side), :
             ].astype(jnp.bfloat16)
-
-
-def dft(blocks, frame_len):
-    first, twist, last = dft_tables(frame_len)
-    rows, side = blocks[0].shape[0], FACTOR_A
-    whole = lambda *shape: pl.BlockSpec(shape, lambda i: (0,) * len(shape))
-    return pl.pallas_call(
-        dft_kernel,
-        grid=(rows // ROWS,),
-        in_specs=[pl.BlockSpec((ROWS, side, side), lambda i: (i, 0, 0))] * 2
-        + [whole(2 * side, 2 * side), whole(2, side, side), whole(2 * side, 2 * side)],
-        out_specs=pl.BlockSpec((side, ROWS, 2 * side), lambda i: (0, i, 0)),
-        out_shape=jax.ShapeDtypeStruct((side, rows, 2 * side), jnp.bfloat16),
-        scratch_shapes=[pltpu.VMEM((2, ROWS * side, side), jnp.float32)],
-        compiler_params=pltpu.CompilerParams(vmem_limit_bytes=40 * 2**20),
-    )(*blocks, jnp.asarray(first), jnp.asarray(twist), jnp.asarray(last))
 
 
 def correlate_kernel(scale, rows, flag_ref, all_ref, out_ref):
@@ -165,14 +151,19 @@
     own_real = all_ref[0, 0, pl.ds(start, rows), :] * flags
     own_imag = all_ref[0, 1, pl.ds(start, rows), :] * flags
     columns = jnp.concatenate([all_ref[0, 0], all_ref[0, 1]], axis=1)
-    for part, own in enumerate(((own_real, own_imag), (own_imag, -own_real))):
-        total = lax.dot_general(
-            jnp.concatenate(own, axis=1),
-            columns,
-            (((1,), (1,)), ((), ())),
-            preferred_element_type=jnp.float32,
-        )
-        out_ref[0, part, 0] = (total * scale).astype(jnp.bfloat16)
+    own = jnp.concatenate(
+        [
+            jnp.concatenate([own_real, own_imag], axis=1),
+            jnp.concatenate([own_imag, -own_real], axis=1),
+        ],
+        axis=0,
+    )
+    total = lax.dot_general(
+        own, columns, (((1,), (1,)), ((), ())), preferred_element_type=jnp.float32
+    )
+    total = (total * scale).astype(jnp.bfloat16)
+    out_ref[0, 0, 0] = total[:rows]
+    out_ref[0, 1, 0] = total[rows:]
 
 
 def correlate_bins(gathered, flags, rows, scale):
@@ -190,15 +181,18 @@
     )(flags, gathered)
 
 
-def move_kernel(wide, chunks, spectra, gathered, local_sem, z_send, z_recv, x_send, x_recv,
-                pair_send, pair_recv, last_send, last_recv):
+def move_kernel(wide, x0_ref, x1_ref, first_ref, twist_ref, last_ref, gathered, flip, spectra,
+                local_sem, z_send, z_recv, x_send, x_recv, pair_send, pair_recv, last_send,
+                last_recv):
     me = lax.axis_index("wide")
     panel = lax.axis_index("narrow")
     pair = panel + 1 - 2 * lax.rem(panel, 2)
     across = lax.rem(panel + 2, 4)
     across_pair = lax.rem(pair + 2, 4)
-    rows = spectra.shape[3]
-    size = spectra.shape[1] // chunks
+    rows = x0_ref.shape[0]
+    row_chunks = rows // ROWS
+    chunks = row_chunks * GROUPS
+    size = spectra.shape[2] // GROUPS
 
     barrier = pltpu.get_barrier_semaphore()
     peers = [{"wide": lax.rem(me + step, wide)} for step in range(1, wide)]
@@ -208,11 +202,14 @@
     pl.semaphore_wait(barrier, len(peers))
 
     def spot(chunk, owner, source):
-        start = pl.multiple_of((owner * wide + source) * rows, rows)
-        return gathered.at[pl.ds(chunk * size, size), :, pl.ds(start, rows), :]
+        start = (owner * wide + source) * rows + chunk // GROUPS * ROWS
+        group = chunk % GROUPS
+        start = pl.multiple_of(start, ROWS)
+        return gathered.at[pl.ds(group * size, size), :, pl.ds(start, ROWS), :]
 
     def mine(target, chunk):
-        return spectra.at[target, pl.ds(chunk * size, size)]
+        group = chunk % GROUPS
+        return spectra.at[chunk // GROUPS, target, pl.ds(group * size, size)]
 
     def remote(src, dst, send, recv, peer):
         return pltpu.make_async_remote_copy(
@@ -284,25 +281,38 @@
             second_hop(chunk, step, True).wait_recv()
         return carry
 
-    lax.fori_loop(0, chunks, begin, 0)
+    def transform(row_chunk, carry):
+        tables = (first_ref, twist_ref, last_ref)
+        dft_chunk((x0_ref, x1_ref), row_chunk, tables, flip, spectra)
+        return lax.fori_loop(row_chunk * GROUPS, (row_chunk + 1) * GROUPS, begin, carry)
+
+    lax.fori_loop(0, row_chunks, transform, 0)
     onward(0, 0)
     lax.fori_loop(1, chunks, both, 0)
     relay(chunks - 1, 0)
     lax.fori_loop(0, chunks, finish, 0)
 
 
-def move(spectra, wide, narrow):
-    bins, parts, rows, depth = spectra.shape[1:]
-    chunks = CHUNKS
-    table = pltpu.SemaphoreType.DMA((chunks, wide))
+def move(blocks, frame_len, wide, narrow, bins):
+    first, twist, last = dft_tables(frame_len)
+    rows, side = blocks[0].shape[0], FACTOR_A
+    row_chunks = rows // ROWS
+    table = pltpu.SemaphoreType.DMA((row_chunks * GROUPS, wide))
     return pl.pallas_call(
-        functools.partial(move_kernel, wide, chunks),
-        in_specs=[pl.BlockSpec(memory_space=pl.ANY)],
+        functools.partial(move_kernel, wide),
+        in_specs=[pl.BlockSpec(memory_space=pltpu.VMEM)] * 5,
         out_specs=pl.BlockSpec(memory_space=pl.ANY),
-        out_shape=jax.ShapeDtypeStruct((bins, parts, narrow * wide * rows, depth), jnp.bfloat16),
-        scratch_shapes=[pltpu.SemaphoreType.DMA((chunks,))] + [table] * 8,
-        compiler_params=pltpu.CompilerParams(collective_id=0, has_side_effects=True),
-    )(spectra)
+        out_shape=jax.ShapeDtypeStruct((bins, 2, narrow * wide * rows, 2 * side), jnp.bfloat16),
+        scratch_shapes=[
+            pltpu.VMEM((2, ROWS * side, side), jnp.float32),
+            pltpu.VMEM((row_chunks, wide, bins, 2, ROWS, 2 * side), jnp.bfloat16),
+            pltpu.SemaphoreType.DMA((row_chunks * GROUPS,)),
+        ]
+        + [table] * 8,
+        compiler_params=pltpu.CompilerParams(
+            collective_id=0, has_side_effects=True, vmem_limit_bytes=32 * 2**20
+        ),
+    )(*blocks, jnp.asarray(first), jnp.asarray(twist), jnp.asarray(last))
 
 
 def filter_rows(voltages, fir_coeffs, spectrum):
@@ -323,8 +333,7 @@
     local_bins = channel_keep_flags.shape[0] // bin_width
     filtered = [filter_rows(voltages[0], fir_coeffs, s) for s in range(spectrum_count)]
     blocks = [lax.optimization_barrier(x).reshape(inputs_here, FACTOR_A, FACTOR_A) for x in filtered]
-    spectra = dft(blocks, frame_len).reshape(wide, local_bins, 2, inputs_here, 2 * bin_width)
-    gathered = move(spectra, wide, 4)
+    gathered = move(blocks, frame_len, wide, 4, local_bins)
     flags = channel_keep_flags.astype(jnp.bfloat16).reshape(local_bins, 1, bin_width)
     flags = jnp.concatenate([flags] * spectrum_count, axis=2)
     scale = 1.0 / (spectrum_count * bin_width)
@@ -340,7 +349,7 @@
         rows = voltages.shape[1]
         spectrum_count = voltages.shape[2] // frame_len - tap_count + 1
         fits = frame_len == FACTOR_A**2 and rows % ROWS == 0 and spectrum_count == 2
-        bins_fit = channel_keep_flags.shape[0] // FACTOR_A % CHUNKS == 0
+        bins_fit = channel_keep_flags.shape[0] // FACTOR_A % GROUPS == 0
         if fits and bins_fit and narrow == 4 and wide == 4:
             return fast_body(wide, voltages, fir_coeffs, channel_keep_flags)
         return plain_body(voltages, fir_coeffs, channel_keep_flags)

time: 164 us -> 157 us (0.957)
  Pallas kernels: 153 us -> 141 us
  local copies, waits for them, and re-layouts: 5.01 us -> 8.72 us
    pallas_call x2 -> x1, Pallas kernels: 132 us -> 121 us  [move(): pl.pallas_call(functools.partial(move_kernel, wide), in_specs=[pl.BlockSp...]
    unnamed x10, local copies, waits for them, and re-layouts: 3.18 us -> 6.88 us
where the time goes in v3:
time: 157 us; the launch traced here: 156 us
  Pallas kernels  141 us (90%)
  local copies, waits for them, and re-layouts  8.72 us (6%)
  other arithmetic  6.11 us (4%)
    pallas_call x1, Pallas kernels, move(): pl.pallas_call(functools.partial(move_kernel, wide), in_specs=[pl.BlockSp...  121 us
    pallas_call x1, Pallas kernels, correlate_bins(): pl.pallas_call(functools.partial(correlate_kernel, scale, rows), grid=(bi...  20.8 us
    unnamed x10, local copies, waits for them, and re-layouts  6.88 us
    convert_element_type x1, other arithmetic, filter_rows(): return total.astype(jnp.bfloat16)  5.39 us

profile of v3, /device:TPU:17, one launch (start us, length us, event | category | flops | bytes accessed | tf_op | source)
XLA Modules:
  0.0 156.3 jit_solution(4277799997389901699)
XLA Ops:
  0.0 0.7 convert_bitcast_fusion
  0.7 1.8 %fusion.8 = (f32[1,16384]{1,0:T(1,128)S(1)}, f32[1,16384]{1,0:T(1,128)S(1)}, f32[1,16384]{1,0:T(1,128)S(1)}, f32[1,16384]{1,0:T(1,128)S(1)}) fusion(f32[4,16384]{1,0:T(4,128)} %param.7), kind=kLoop, calls=%fused_computation.16 | loop fusion | bytes 524288 | tf_op jit(solution)/shard_map/slice | solution.py:324
  2.6 5.4 %fusion.7 = (bf16[64,16384]{1,0:T(8,128)(2,1)S(1)}, bf16[64,16384]{1,0:T(8,128)(2,1)S(1)}) fusion(bf16[64,81920]{1,0:T(8,128)(2,1)} %bitcast.13, f32[16384]{0:T(1024)S(1)} %bitcast.18, f32[16384]{0:T(1024)S(1)} %bitcast.19, f32[16384]{0:T(1024)S(1)} %bitcast.17, f32[16384]{0:T(1024)S(1)} %bitcast.16), kind=kLoop, calls=%fused_computation.13 | loop fusion | flops 22020096 | bytes 14942208 | tf_op jit(solution)/shard_map/convert_element_type | solution.py:325
  8.0 0.0 copy-start.1
  8.0 0.0 copy-start.2
  8.0 0.0 copy-start.3
  8.0 0.6 copy.10
  8.6 0.6 copy.9
  9.2 0.0 copy-done.1
  9.2 0.0 copy-done.2
  9.2 0.0 copy-done.3
  9.2 120.6 %shard_map.64.all_ref = bf16[16,2,1024,256]{3,2,1,0:T(8,128)(2,1)S(1)} custom-call(bf16[64,128,128]{2,1,0:T(8,128)(2,1)S(1)} %bitcast.12, bf16[64,128,128]{2,1,0:T(8,128)(2,1)S(1)} %bitcast.11, bf16[256,256]{1,0:T(8,128)(2,1)S(1)} %copy-done.3, f32[2,128,128]{2,1,0:T(8,128)S(1)} %copy-done.2, bf16[256,256]{1,0:T(8,128)(2,1)S(1)} %copy-done.1), custom_call_target="tpu_custom_call" | custom-call | tf_op jit(solution)/shard_map/pallas_call | solution.py:301
  129.8 0.0 copy-start
  129.8 5.7 %copy-done = bf16[16,2,1024,256]{3,2,1,0:T(8,128)(2,1)} copy-done((bf16[16,2,1024,256]{3,2,1,0:T(8,128)(2,1)}, bf16[16,2,1024,256]{3,2,1,0:T(8,128)(2,1)S(1)}, u32[]{:S(2)}) %copy-start) | copy-done | bytes 16777240
  135.5 20.8 %shard_map.65 = bf16[16,2,1,256,1024]{4,3,2,1,0:T(8,128)(2,1)} custom-call(bf16[16,1,256]{2,1,0:T(2,128)(2,1)S(1)} %pad_maximum_fusion.flag_ref, bf16[16,2,1024,256]{3,2,1,0:T(8,128)(2,1)} %copy-done), custom_call_target="tpu_custom_call" | custom-call | tf_op jit(solution)/shard_map/pallas_call | solution.py:171
  (2 shorter events, 0.0 us)
Async XLA Ops:
  8.0 1.2 copy-start.1
  8.0 1.2 copy-start.2
  8.0 1.2 copy-start.3
  129.8 5.7 %copy-start = (bf16[16,2,1024,256]{3,2,1,0:T(8,128)(2,1)}, bf16[16,2,1024,256]{3,2,1,0:T(8,128)(2,1)S(1)}, u32[]{:S(2)}) copy-start(bf16[16,2,1024,256]{3,2,1,0:T(8,128)(2,1)S(1)} %shard_map.64.all_ref) | copy-start | bytes 50331652

commit v4 on v3

--- a/solution.py
+++ b/solution.py
@@ -79,6 +79,7 @@
 
 ROWS = 16
 GROUPS = 4
+COLUMNS = 256
 ORDER = (2, 1, 3)
 
 
@@ -150,7 +151,6 @@
     flags = flag_ref[0]
     own_real = all_ref[0, 0, pl.ds(start, rows), :] * flags
     own_imag = all_ref[0, 1, pl.ds(start, rows), :] * flags
-    columns = jnp.concatenate([all_ref[0, 0], all_ref[0, 1]], axis=1)
     own = jnp.concatenate(
         [
             jnp.concatenate([own_real, own_imag], axis=1),
@@ -158,12 +158,15 @@
         ],
         axis=0,
     )
-    total = lax.dot_general(
-        own, columns, (((1,), (1,)), ((), ())), preferred_element_type=jnp.float32
-    )
-    total = (total * scale).astype(jnp.bfloat16)
-    out_ref[0, 0, 0] = total[:rows]
-    out_ref[0, 1, 0] = total[rows:]
+    for first in range(0, all_ref.shape[2], COLUMNS):
+        span = slice(first, first + COLUMNS)
+        columns = jnp.concatenate([all_ref[0, 0, span, :], all_ref[0, 1, span, :]], axis=1)
+        total = lax.dot_general(
+            own, columns, (((1,), (1,)), ((), ())), preferred_element_type=jnp.float32
+        )
+        total = (total * scale).astype(jnp.bfloat16)
+        out_ref[0, 0, 0, :, span] = total[:rows]
+        out_ref[0, 1, 0, :, span] = total[rows:]
 
 
 def correlate_bins(gathered, flags, rows, scale):
@@ -177,7 +180,7 @@
         ],
         out_specs=pl.BlockSpec((1, parts, 1, rows, inputs), lambda b: (b, 0, 0, 0, 0)),
         out_shape=jax.ShapeDtypeStruct((bins, parts, 1, rows, inputs), jnp.bfloat16),
-        compiler_params=pltpu.CompilerParams(vmem_limit_bytes=40 * 2**20),
+        compiler_params=pltpu.CompilerParams(vmem_limit_bytes=20 * 2**20),
     )(flags, gathered)
 
 

time: 157 us -> 145 us (0.924)
  Pallas kernels: 141 us -> 135 us
  local copies, waits for them, and re-layouts: 8.72 us -> 2.92 us
    pallas_call x1, Pallas kernels: 20.8 us -> 14.5 us  [correlate_bins(): pl.pallas_call(functools.partial(correlate_kernel, scale, rows), grid=(bi...]
    unnamed x10 -> x8, local copies, waits for them, and re-layouts: 6.88 us -> 1.17 us
where the time goes in v4:
time: 145 us; the launch traced here: 144 us
  Pallas kernels  135 us (93%)
  other arithmetic  6.11 us (4%)
  local copies, waits for them, and re-layouts  2.92 us (2%)
    pallas_call x1, Pallas kernels, move(): pl.pallas_call(functools.partial(move_kernel, wide), in_specs=[pl.BlockSp...  121 us
    pallas_call x1, Pallas kernels, correlate_bins(): pl.pallas_call(functools.partial(correlate_kernel, scale, rows), grid=(bi...  14.5 us
    convert_element_type x1, other arithmetic, filter_rows(): return total.astype(jnp.bfloat16)  5.39 us

profile of v4, /device:TPU:17, one launch (start us, length us, event | category | flops | bytes accessed | tf_op | source)
XLA Modules:
  0.0 144.3 jit_solution(9684427963587779680)
XLA Ops:
  0.0 0.7 convert_bitcast_fusion
  0.7 1.7 %fusion.8 = (f32[1,16384]{1,0:T(1,128)S(1)}, f32[1,16384]{1,0:T(1,128)S(1)}, f32[1,16384]{1,0:T(1,128)S(1)}, f32[1,16384]{1,0:T(1,128)S(1)}) fusion(f32[4,16384]{1,0:T(4,128)} %param.7), kind=kLoop, calls=%fused_computation.16 | loop fusion | bytes 524288 | tf_op jit(solution)/shard_map/slice | solution.py:327
  2.5 5.4 %fusion.7 = (bf16[64,16384]{1,0:T(8,128)(2,1)S(1)}, bf16[64,16384]{1,0:T(8,128)(2,1)S(1)}) fusion(bf16[64,81920]{1,0:T(8,128)(2,1)} %bitcast.13, f32[16384]{0:T(1024)S(1)} %bitcast.18, f32[16384]{0:T(1024)S(1)} %bitcast.19, f32[16384]{0:T(1024)S(1)} %bitcast.17, f32[16384]{0:T(1024)S(1)} %bitcast.16), kind=kLoop, calls=%fused_computation.13 | loop fusion | flops 22020096 | bytes 14942208 | tf_op jit(solution)/shard_map/convert_element_type | solution.py:328
  7.9 0.0 copy-start
  7.9 0.0 copy-start.1
  7.9 0.0 copy-start.2
  7.9 0.6 copy.10
  8.5 0.6 copy.9
  9.1 0.0 copy-done
  9.1 0.0 copy-done.1
  9.1 0.0 copy-done.2
  9.1 120.6 %shard_map.64.all_ref = bf16[16,2,1024,256]{3,2,1,0:T(8,128)(2,1)S(1)} custom-call(bf16[64,128,128]{2,1,0:T(8,128)(2,1)S(1)} %bitcast.12, bf16[64,128,128]{2,1,0:T(8,128)(2,1)S(1)} %bitcast.11, bf16[256,256]{1,0:T(8,128)(2,1)S(1)} %copy-done.2, f32[2,128,128]{2,1,0:T(8,128)S(1)} %copy-done.1, bf16[256,256]{1,0:T(8,128)(2,1)S(1)} %copy-done), custom_call_target="tpu_custom_call" | custom-call | tf_op jit(solution)/shard_map/pallas_call | solution.py:304
  129.7 14.5 %shard_map.65 = bf16[16,2,1,256,1024]{4,3,2,1,0:T(8,128)(2,1)} custom-call(bf16[16,1,256]{2,1,0:T(2,128)(2,1)S(1)} %pad_maximum_fusion.flag_ref, bf16[16,2,1024,256]{3,2,1,0:T(8,128)(2,1)S(1)} %shard_map.64.all_ref), custom_call_target="tpu_custom_call" | custom-call | tf_op jit(solution)/shard_map/pallas_call | solution.py:174
  (2 shorter events, 0.0 us)
Async XLA Ops:
  7.9 1.2 copy-start
  7.9 1.2 copy-start.1
  7.9 1.2 copy-start.2

commit v5 on v4

--- a/solution.py
+++ b/solution.py
@@ -80,7 +80,6 @@
 ROWS = 16
 GROUPS = 4
 COLUMNS = 256
-ORDER = (2, 1, 3)
 
 
 def split_table(table):
@@ -248,7 +247,8 @@
 
     def begin(chunk, carry):
         first_hop(chunk, 0, False).start()
-        for step in ORDER:
+        near = 1 + 2 * lax.rem(me, 2)
+        for step in (2, 4 - near, near):
             along(chunk, step).start()
         first_hop(chunk, 0, True).start()
         pltpu.make_async_copy(mine(me, chunk), spot(chunk, panel, me), local_sem.at[chunk]).start()

time: 145 us -> 145 us (level)
  no operation moved by 1% of the time
where the time goes in v5:
time: 145 us; the launch traced here: 144 us
  Pallas kernels  135 us (93%)
  other arithmetic  6.11 us (4%)
  local copies, waits for them, and re-layouts  2.92 us (2%)
    pallas_call x1, Pallas kernels, move(): pl.pallas_call(functools.partial(move_kernel, wide), in_specs=[pl.BlockSp...  121 us
    pallas_call x1, Pallas kernels, correlate_bins(): pl.pallas_call(functools.partial(correlate_kernel, scale, rows), grid=(bi...  14.6 us
    convert_element_type x1, other arithmetic, filter_rows(): return total.astype(jnp.bfloat16)  5.39 us

profile of v5, /device:TPU:17, one launch (start us, length us, event | category | flops | bytes accessed | tf_op | source)
XLA Modules:
  0.0 144.3 jit_solution(2651787424599160787)
XLA Ops:
  0.0 0.7 convert_bitcast_fusion
  0.7 1.7 %fusion.8 = (f32[1,16384]{1,0:T(1,128)S(1)}, f32[1,16384]{1,0:T(1,128)S(1)}, f32[1,16384]{1,0:T(1,128)S(1)}, f32[1,16384]{1,0:T(1,128)S(1)}) fusion(f32[4,16384]{1,0:T(4,128)} %param.7), kind=kLoop, calls=%fused_computation.16 | loop fusion | bytes 524288 | tf_op jit(solution)/shard_map/slice | solution.py:327
  2.5 5.4 %fusion.7 = (bf16[64,16384]{1,0:T(8,128)(2,1)S(1)}, bf16[64,16384]{1,0:T(8,128)(2,1)S(1)}) fusion(bf16[64,81920]{1,0:T(8,128)(2,1)} %bitcast.13, f32[16384]{0:T(1024)S(1)} %bitcast.18, f32[16384]{0:T(1024)S(1)} %bitcast.19, f32[16384]{0:T(1024)S(1)} %bitcast.17, f32[16384]{0:T(1024)S(1)} %bitcast.16), kind=kLoop, calls=%fused_computation.13 | loop fusion | flops 22020096 | bytes 14942208 | tf_op jit(solution)/shard_map/convert_element_type | solution.py:328
  7.9 0.0 copy-start
  7.9 0.0 copy-start.1
  7.9 0.0 copy-start.2
  7.9 0.6 copy.10
  8.5 0.6 copy.9
  9.1 0.0 copy-done
  9.1 0.0 copy-done.1
  9.1 0.0 copy-done.2
  9.1 120.6 %shard_map.64.all_ref = bf16[16,2,1024,256]{3,2,1,0:T(8,128)(2,1)S(1)} custom-call(bf16[64,128,128]{2,1,0:T(8,128)(2,1)S(1)} %bitcast.12, bf16[64,128,128]{2,1,0:T(8,128)(2,1)S(1)} %bitcast.11, bf16[256,256]{1,0:T(8,128)(2,1)S(1)} %copy-done.2, f32[2,128,128]{2,1,0:T(8,128)S(1)} %copy-done.1, bf16[256,256]{1,0:T(8,128)(2,1)S(1)} %copy-done), custom_call_target="tpu_custom_call" | custom-call | tf_op jit(solution)/shard_map/pallas_call | solution.py:304
  129.7 14.6 %shard_map.65 = bf16[16,2,1,256,1024]{4,3,2,1,0:T(8,128)(2,1)} custom-call(bf16[16,1,256]{2,1,0:T(2,128)(2,1)S(1)} %pad_maximum_fusion.flag_ref, bf16[16,2,1024,256]{3,2,1,0:T(8,128)(2,1)S(1)} %shard_map.64.all_ref), custom_call_target="tpu_custom_call" | custom-call | tf_op jit(solution)/shard_map/pallas_call | solution.py:173
  (2 shorter events, 0.0 us)
Async XLA Ops:
  7.9 1.2 copy-start
  7.9 1.2 copy-start.1
  7.9 1.2 copy-start.2

commit v6 on v5

--- a/solution.py
+++ b/solution.py
@@ -78,7 +78,7 @@
 
 
 ROWS = 16
-GROUPS = 4
+GROUPS = 2
 COLUMNS = 256
 
 

time: 145 us -> 146 us (level)
  no operation moved by 1% of the time
where the time goes in v6:
time: 146 us
  Pallas kernels  136 us (93%)
  other arithmetic  6.11 us (4%)
  local copies, waits for them, and re-layouts  2.92 us (2%)
    pallas_call x1, Pallas kernels, move(): pl.pallas_call(functools.partial(move_kernel, wide), in_specs=[pl.BlockSp...  122 us
    pallas_call x1, Pallas kernels, correlate_bins(): pl.pallas_call(functools.partial(correlate_kernel, scale, rows), grid=(bi...  14.5 us
    convert_element_type x1, other arithmetic, filter_rows(): return total.astype(jnp.bfloat16)  5.39 us

profile of v6, /device:TPU:17, one launch (start us, length us, event | category | flops | bytes accessed | tf_op | source)
XLA Modules:
  0.0 145.5 jit_solution(2112747268768987567)
XLA Ops:
  0.0 0.7 convert_bitcast_fusion
  0.7 1.7 %fusion.8 = (f32[1,16384]{1,0:T(1,128)S(1)}, f32[1,16384]{1,0:T(1,128)S(1)}, f32[1,16384]{1,0:T(1,128)S(1)}, f32[1,16384]{1,0:T(1,128)S(1)}) fusion(f32[4,16384]{1,0:T(4,128)} %param.7), kind=kLoop, calls=%fused_computation.16 | loop fusion | bytes 524288 | tf_op jit(solution)/shard_map/slice | solution.py:327
  2.5 5.4 %fusion.7 = (bf16[64,16384]{1,0:T(8,128)(2,1)S(1)}, bf16[64,16384]{1,0:T(8,128)(2,1)S(1)}) fusion(bf16[64,81920]{1,0:T(8,128)(2,1)} %bitcast.13, f32[16384]{0:T(1024)S(1)} %bitcast.18, f32[16384]{0:T(1024)S(1)} %bitcast.19, f32[16384]{0:T(1024)S(1)} %bitcast.17, f32[16384]{0:T(1024)S(1)} %bitcast.16), kind=kLoop, calls=%fused_computation.13 | loop fusion | flops 22020096 | bytes 14942208 | tf_op jit(solution)/shard_map/convert_element_type | solution.py:328
  7.9 0.0 copy-start
  7.9 0.0 copy-start.1
  7.9 0.0 copy-start.2
  7.9 0.6 copy.10
  8.5 0.6 copy.9
  9.1 0.0 copy-done
  9.1 0.0 copy-done.1
  9.1 0.0 copy-done.2
  9.1 121.9 %shard_map.64.all_ref = bf16[16,2,1024,256]{3,2,1,0:T(8,128)(2,1)S(1)} custom-call(bf16[64,128,128]{2,1,0:T(8,128)(2,1)S(1)} %bitcast.12, bf16[64,128,128]{2,1,0:T(8,128)(2,1)S(1)} %bitcast.11, bf16[256,256]{1,0:T(8,128)(2,1)S(1)} %copy-done.2, f32[2,128,128]{2,1,0:T(8,128)S(1)} %copy-done.1, bf16[256,256]{1,0:T(8,128)(2,1)S(1)} %copy-done), custom_call_target="tpu_custom_call" | custom-call | tf_op jit(solution)/shard_map/pallas_call | solution.py:304
  131.0 14.5 %shard_map.65 = bf16[16,2,1,256,1024]{4,3,2,1,0:T(8,128)(2,1)} custom-call(bf16[16,1,256]{2,1,0:T(2,128)(2,1)S(1)} %pad_maximum_fusion.flag_ref, bf16[16,2,1024,256]{3,2,1,0:T(8,128)(2,1)S(1)} %shard_map.64.all_ref), custom_call_target="tpu_custom_call" | custom-call | tf_op jit(solution)/shard_map/pallas_call | solution.py:173
  (2 shorter events, 0.0 us)
Async XLA Ops:
  7.9 1.2 copy-start
  7.9 1.2 copy-start.1
  7.9 1.2 copy-start.2
